TPU v7x, 512 devices: a whole 4x4x16 slice. The times are simulated.
512 devices in a mesh: section: 8 (over z_hi, core), dp: 64 (over y, x, z_lo).
Axes of the slice: x: 4, y: 4, z: 16 (z_hi: 4, z_lo: 4; z = z_hi * 4 + z_lo), core: 2. Of those that a mesh axis runs over, the one named last changes fastest.
Arguments:
- inputs: bfloat16 [2, 4096, 512], P(None, 'dp'), may hold values from -24 to 24
- weights: bfloat16 [8, 1, 512, 512], P('section'), may hold values from -0.125 to 0.125
- cotangent: bfloat16 [2, 4096, 512], P(None, 'dp'), may hold values from -24 to 24
Outputs:
- precond: float32 [8, 1, 512, 512], P('section', None, 'dp')
All inputs are finite; a program needn't handle non-finite values.
Results may differ from a plain program's by a relative error of at most 0.01105.
Values may be sent and summed in bfloat16 or wider, within the bound.
A program may use at most 64 MiB of HBM per device.

v0:
```python
import jax
import jax.numpy as jnp
from jax import lax
from jax.sharding import PartitionSpec as P

gelu_coef = 0.7978845608
cubic_coef = 0.044715
damping_level = 0.1
loss_scale = 0.0078125


def passed_along(value, axis, steps):
    count = lax.axis_size(axis)
    initial, last = (max(0, -steps), min(count, count - steps))
    return lax.ppermute(value, axis, [(source, source + steps) for source in range(initial, last)])


def gelu_value(values):
    argument = gelu_coef * (values + cubic_coef * values * values * values)
    return 0.5 * values * (1.0 + jnp.tanh(argument))


def gelu_slope(values):
    argument = gelu_coef * (values + cubic_coef * values * values * values)
    tangent = jnp.tanh(argument)
    return 0.5 * (1.0 + tangent) + 0.5 * values * (1.0 - tangent * tangent) * gelu_coef * (
        1.0 + 3.0 * cubic_coef * values * values
    )


def chol_solve(lower_factor, right_side):
    middle = lax.linalg.triangular_solve(lower_factor, right_side, left_side=True, lower=True)
    return lax.linalg.triangular_solve(
        lower_factor, middle, left_side=True, lower=True, transpose_a=True
    )


def damped_factor(matrix):
    order_size = matrix.shape[-1]
    return jnp.linalg.cholesky(matrix + damping_level * jnp.eye(order_size, dtype=matrix.dtype))


def section_forward(current, weight_stack):
    preact = jnp.dot(current, weight_stack[0], preferred_element_type=jnp.float32)
    level_inputs = [current]
    level_preacts = [preact]
    current = (current.astype(jnp.float32) + gelu_value(preact)).astype(jnp.bfloat16)
    return (current, jnp.stack(level_inputs), jnp.stack(level_preacts))


def section_backward(upstream, weight_stack, preacts):
    level_count = weight_stack.shape[0]
    level_grads = [None] * level_count
    for level_index in reversed(range(level_count)):
        grad_pre = (upstream.astype(jnp.float32) * gelu_slope(preacts[level_index])).astype(
            jnp.bfloat16
        )
        level_grads[level_index] = grad_pre
        upstream = (
            upstream.astype(jnp.float32)
            + jnp.dot(grad_pre, weight_stack[level_index].T, preferred_element_type=jnp.float32)
        ).astype(jnp.bfloat16)
    return (upstream, jnp.stack(level_grads))


def body(inputs, weights, cotangent):
    micro_count, tok_rows, features = inputs.shape
    weight_stack = weights[0]
    levels = weight_stack.shape[0]
    section_count = lax.axis_size("section")
    position = lax.axis_index("section")
    is_first = position == 0
    is_last = position == section_count - 1
    scaled_top = cotangent * loss_scale
    source = inputs.reshape(micro_count * tok_rows, features)
    current = jnp.where(is_first, source, jnp.zeros_like(source))
    for step_index in range(section_count - 1):
        produced, _, _ = section_forward(current, weight_stack)
        arrived = passed_along(produced, "section", 1)
        current = jnp.where(is_first, source, arrived)
    _, saved_in, saved_pre = section_forward(current, weight_stack)
    top_grad = scaled_top.reshape(micro_count * tok_rows, features)
    upstream = jnp.where(is_last, top_grad, jnp.zeros_like(top_grad))
    for step_index in range(section_count - 1):
        passed, _ = section_backward(upstream, weight_stack, saved_pre)
        arrived = passed_along(passed, "section", -1)
        upstream = jnp.where(is_last, top_grad, arrived)
    _, saved_grad = section_backward(upstream, weight_stack, saved_pre)
    token_total = micro_count * tok_rows * lax.axis_size("dp")
    act_gram = (
        jnp.einsum("lrb,lrc->lbc", saved_in, saved_in, preferred_element_type=jnp.float32)
        / token_total
    )
    grad_gram = jnp.einsum(
        "lrb,lrc->lbc", saved_grad, saved_grad, preferred_element_type=jnp.float32
    )
    weight_grad = jnp.einsum(
        "lrb,lrc->lbc", saved_in, saved_grad, preferred_element_type=jnp.float32
    )
    act_sum, grad_sum = lax.psum((act_gram, grad_gram), "dp")
    act_lower = damped_factor(act_sum)
    grad_lower = damped_factor(grad_sum)
    shard_rows = features // lax.axis_size("dp")
    row_offset = lax.axis_index("dp") * shard_rows
    grad_rows = lax.psum_scatter(weight_grad, "dp", scatter_dimension=1, tiled=True)
    half_rows = jnp.swapaxes(chol_solve(grad_lower, jnp.swapaxes(grad_rows, 1, 2)), 1, 2)
    selector = (
        lax.broadcasted_iota(jnp.int32, (features, shard_rows), 0)
        == row_offset + lax.broadcasted_iota(jnp.int32, (features, shard_rows), 1)
    ).astype(jnp.float32)
    inverse_cols = chol_solve(act_lower, jnp.broadcast_to(selector, (levels, features, shard_rows)))
    inverse_rows = jnp.swapaxes(inverse_cols, 1, 2)
    result = jnp.einsum(
        "lrk,lkc->lrc",
        inverse_rows,
        lax.all_gather(half_rows, "dp", axis=1, tiled=True),
        precision=lax.Precision.HIGHEST,
    )
    return result[None]


def solution(mesh):
    placed = (P(None, "dp", None), P("section", None, None, None), P(None, "dp", None))
    return jax.shard_map(
        body, mesh=mesh, in_specs=placed, out_specs=P("section", None, "dp", None), check_vma=False
    )
```

profile of v0, /device:TPU:32, one launch (start us, length us, event | category | flops | bytes accessed | tf_op | source)
XLA Modules:
  0.0 1641.3 jit_solution(4442230447276924731)
XLA Ops:
  11.0 11.3 collective-permute-start.1
  23.6 9.5 collective-permute-start.2
  88.7 9.6 collective-permute-done.8
  110.6 9.8 collective-permute-done.10
  157.2 737.7 %all-reduce.4.cloned.1.call-done = (f32[1,512,512]{1,2,0:T(8,128)}, f32[1,512,512]{1,2,0:T(8,128)}) async-done(((f32[1,512,512]{1,2,0:T(8,128)}, f32[1,512,512]{1,2,0:T(8,128)}), (f32[1,512,512]{1,2,0:T(8,128)}, f32[1,512,512]{1,2,0:T(8,128)})) %all-reduce.4.cloned.1.call-update) | async-done | bytes 2097168 | tf_op jit(solution)/shard_map/psum | solution.py:100
  901.0 11.7 custom-call.39
  912.9 9.8 custom-call.40
  923.4 11.7 custom-call.41
  935.1 10.2 custom-call.42
  946.0 11.7 custom-call.43
  957.7 9.8 custom-call.44
  971.6 11.9 custom-call.48
  983.6 9.8 custom-call.49
  996.0 11.7 custom-call.50
  1009.0 9.8 custom-call.51
  1020.4 11.9 custom-call.52
  1033.0 9.8 custom-call.53
  1044.3 11.7 custom-call.54
  1061.9 11.7 custom-call.45
  1073.7 11.6 while.9
  1085.3 39.3 %custom-call.56 = f32[1,4,128,128]{2,3,1,0:T(8,128)S(1)} custom-call(f32[1,4,128,128]{3,2,1,0:T(8,128)S(1)} %bitcast.502), custom_call_target="InvertDiagBlocksLowerTriangular" | custom-call | tf_op jit(solution)/shard_map/triangular_solve/custom-call.8 | solution.py:33
  1127.2 143.2 %reduce-scatter.2.cloned.1.call-done = f32[1,8,512]{2,1,0:T(8,128)} async-done(((f32[1,512,512]{2,1,0:T(8,128)}), f32[1,8,512]{2,1,0:T(8,128)}) %reduce-scatter.2.cloned.1.call-update) | async-done | bytes 16400 | tf_op jit(solution)/shard_map/reduce_scatter | solution.py:105
  1290.7 39.3 %custom-call.47 = f32[1,4,128,128]{2,3,1,0:T(8,128)S(1)} custom-call(f32[1,4,128,128]{3,2,1,0:T(8,128)S(1)} %bitcast.501), custom_call_target="InvertDiagBlocksLowerTriangular" | custom-call | tf_op jit(solution)/shard_map/triangular_solve/custom-call.8 | solution.py:33
  1333.0 298.9 %all-gather.2.cloned.1.call-done = f32[1,512,512]{2,1,0:T(8,128)} async-done(((f32[1,8,512]{2,1,0:T(8,128)}), f32[1,512,512]{2,1,0:T(8,128)}) %all-gather.2.cloned.1.call-update) | async-done | bytes 1048592 | tf_op jit(solution)/shard_map/all_gather | solution.py:116
  (186 shorter events, 177.9 us)
Async XLA Ops:
  6.5 1.2 copy-start
  6.5 888.4 %all-reduce.4.cloned.1.call-start = ((), (), s32[]{:S(2)}) async-start(), calls=%async_computation.3 | async-start | bytes 4194304 | tf_op jit(solution)/shard_map/psum | solution.py:100
  6.5 1.0 copy-start.1
  8.0 2.7 collective-permute-start
  11.0 12.2 collective-permute-start.1
  23.6 10.5 collective-permute-start.2
  34.5 10.2 collective-permute-start.3
  45.0 10.2 collective-permute-start.4
  55.2 9.6 copy-start.6
  55.5 10.2 collective-permute-start.5
  66.1 10.2 collective-permute-start.6
  77.0 10.1 collective-permute-start.7
  87.4 10.9 collective-permute-start.8
  98.7 10.2 collective-permute-start.9
  109.3 11.1 collective-permute-start.10
  120.7 10.3 collective-permute-start.11
  131.4 10.2 collective-permute-start.12
  141.9 12.1 collective-permute-start.13
  155.5 1115.0 %reduce-scatter.2.cloned.1.call-start = ((), (), s32[]{:S(2)}) async-start(), calls=%async_computation.1 | async-start | bytes 1064960 | tf_op jit(solution)/shard_map/reduce_scatter | solution.py:105
  156.9 1475.0 %all-gather.2.cloned.1.call-start = ((), (), s32[]{:S(2)}) async-start(), calls=%async_computation.2 | async-start | bytes 1064960 | tf_op jit(solution)/shard_map/all_gather | solution.py:116
  898.1 1.7 copy-start.2
  901.0 21.7 %copy-start.4 = (f32[1,512,512]{2,1,0:T(8,128)S(1)}, f32[1,512,512]{2,1,0:T(8,128)}, u32[]{:S(2)}) copy-start(f32[1,512,512]{2,1,0:T(8,128)} %copy-done.3) | copy-start | bytes 3145732
  970.5 1.0 copy-start.5
  1271.3 1.0 copy-start.7
  (1 other events, 1.0 us)
Sparse Core Ops, SparseCore 0:
  155.6 739.3 all-reduce.3
  897.9 372.4 reduce-scatter.1
  1280.2 351.6 all-gather.1
where the time goes:
time: 1650 us; the launch traced here: 1640 us
  waiting for transfers between devices  1250 us (76%)
  other arithmetic  246 us (15%)
  starting transfers between devices  68.7 us (4%)
  matrix products  31.1 us (2%)
  local copies, waits for them, and re-layouts  25.1 us (2%)
  between operations  19.2 us (1%)
    psum x1, waiting for transfers between devices, body(): act_sum, grad_sum = lax.psum((act_gram, grad_gram), 'dp')  738 us
    all_gather x1, waiting for transfers between devices, body(): lax.all_gather(half_rows, 'dp', axis=1, tiled=True)  299 us
    another operation x30, other arithmetic, damped_factor(): jnp.linalg.cholesky(matrix + damping_level * jnp.eye(order_size, dtype=ma...  159 us
    reduce_scatter x1, waiting for transfers between devices, body(): lax.psum_scatter(weight_grad, 'dp', scatter_dimension=1, tiled=True)  143 us
    another operation x5, other arithmetic, chol_solve(): lax.linalg.triangular_solve(lower_factor, middle, left_side=True, lower=T...  79.9 us
    ppermute x14, waiting for transfers between devices, passed_along(): lax.ppermute(value, axis, [(source, source + steps) for source in range(i...  71.2 us
    ppermute x14, starting transfers between devices, passed_along(): lax.ppermute(value, axis, [(source, source + steps) for source in range(i...  68.5 us
  transfers between devices with their start and end apart: 17, of which 17 were waited for; matrix products, arithmetic and copies ran while one was open for 17% of the time, Pallas kernels for 0%

commit v1 on v0

v1 whole, which is shorter than its diff:
```python
import functools
import jax
import jax.numpy as jnp
from jax import lax
from jax.experimental import pallas as pl
from jax.experimental.pallas import tpu as pltpu
from jax.sharding import PartitionSpec as P

MESH = pl.DeviceIdType.MESH
HIGHEST = lax.Precision.HIGHEST
F32, BF16 = jnp.float32, jnp.bfloat16
gelu_coef = 0.7978845608
cubic_coef = 0.044715
damping_level = 0.1
loss_scale = 0.0078125

STRIDE = {"y": 16, "x": 4, "z": 1}
PAIRS = [(i, j) for i in range(4) for j in range(i, 4)]
ACT_GROUPS = [(0, 5, "xyz"), (5, 5, "yxz")]
GRAD_GROUPS = [(10, 5, "xyz"), (15, 5, "yxz")]
WEIGHT_GROUPS = [(20, 8, "xyz"), (28, 8, "yxz")]
GATHER_AXES = ["yx", "xy"]


class Place:
    def __init__(self):
        self.section = lax.axis_index("section")
        self.dp = lax.axis_index("dp")
        self.core = lax.rem(self.section, 2)
        self.high = lax.div(self.section, 2)
        self.at = {a: lax.rem(lax.div(self.dp, s), 4) for a, s in STRIDE.items()}

    def along(self, axis, delta):
        there = lax.rem(self.at[axis] + delta, 4)
        return there, (self.section, self.dp + (there - self.at[axis]) * STRIDE[axis])

    def other_high(self, delta):
        return (lax.rem(self.high + delta, 4) * 2 + self.core, self.dp)

    def sibling(self):
        return (self.section + 1 - 2 * self.core, self.dp)


def enter(place):
    barrier = pltpu.get_barrier_semaphore()
    peers = [place.sibling()] + [place.other_high(t) for t in range(1, 4)]
    peers += [place.along(a, t)[1] for a in "yxz" for t in range(1, 4)]
    for peer in peers:
        pl.semaphore_signal(barrier, inc=1, device_id=peer, device_id_type=MESH)
    pl.semaphore_wait(barrier, len(peers))


def remote(src, dst, send, recv, peer):
    return pltpu.make_async_remote_copy(
        src_ref=src, dst_ref=dst, send_sem=send, recv_sem=recv, device_id=peer, device_id_type=MESH
    )


def times(index, size):
    return pl.multiple_of(index * size, size)


class Gather:
    def __init__(self, place, own, full, send, recv):
        self.place, self.own, self.full, self.send, self.recv = place, own, full, send, recv
        self.sent = []

    def rows(self, half, coarse):
        last, first = (self.place.at[a] for a in GATHER_AXES[half])
        if coarse:
            return pl.ds(times(last, 128), 128)
        return pl.ds(pl.multiple_of(last * 128 + first * 32, 32), 32)

    def go(self, index, src, dst, peer):
        copy = remote(src, dst, self.send.at[index], self.recv.at[index], peer)
        copy.start()
        self.sent.append(copy)
        return copy

    def run(self):
        place, full = self.place, self.full
        mine = full.at[place.core]
        pending = [[], []]
        for t in (1, 3, 2):
            for half in range(2):
                part = (self.rows(half, False), pl.ds(half * 256, 256))
                pending[half].append(self.go(
                    6 * half + t - 1, self.own.at[part], mine.at[(t, *part)], place.other_high(4 - t)
                ))
        swaps = [self.go(31, self.own, mine.at[0], place.sibling())]
        for phase in range(2):
            for half in range(2):
                for copy in pending[half]:
                    copy.wait_recv()
                block = mine.at[pl.ds(1, 3), self.rows(half, phase == 1), pl.ds(half * 256, 256)]
                axis = GATHER_AXES[half][1 - phase]
                pending[half] = [
                    self.go(6 * half + (3 if phase == 0 else 12) + d - 1, block, block, place.along(axis, d)[1])
                    for d in (1, 3, 2)
                ]
                if phase == 1:
                    swaps.append(self.go(24 + half, block, block, place.sibling()))
        for number, d in enumerate((1, 3, 2)):
            for half in range(2):
                pending[half][number].wait_recv()
                origin = lax.rem(place.at[GATHER_AXES[half][0]] + 4 - d, 4)
                block = mine.at[pl.ds(1, 3), pl.ds(times(origin, 128), 128), pl.ds(half * 256, 256)]
                swaps.append(self.go(26 + half + 6 + 2 * number, block, block, place.sibling()))
        for copy in swaps:
            copy.wait_recv()

    def close(self):
        for copy in self.sent:
            copy.wait_send()


class Sum:
    def __init__(self, place, group, index, part, full, bufs, send, recv):
        self.place, self.index, self.part, self.full = place, index, part, full
        self.first, self.count, self.axes = group
        self.recv1, self.sum1, self.recv2, self.sum2, self.recv3 = bufs
        self.send, self.recv = send, recv
        self.peers = {a: [place.along(a, d) for d in range(1, 4)] for a in self.axes}

    def copies(self, phase):
        blocks, at = pl.ds(self.first, self.count), self.place.at
        a1, a2, a3 = self.axes
        fine = pl.ds(pl.multiple_of(at[a1] * 32 + at[a2] * 8, 8), 8)
        axis = (a1, a2, a3, a2, a1)[phase]
        made = []
        for d, (there, peer) in enumerate(self.peers[axis]):
            if phase == 0:
                src, dst = self.part.at[blocks, pl.ds(times(there, 32), 32)], self.recv1.at[d, blocks]
            elif phase == 1:
                src, dst = self.sum1.at[blocks, pl.ds(times(there, 8), 8)], self.recv2.at[d, blocks]
            elif phase == 2:
                src, dst = self.sum2.at[blocks], self.recv3.at[d, blocks]
            elif phase == 3:
                src = dst = self.full.at[blocks, fine]
            else:
                src = dst = self.full.at[blocks, pl.ds(times(at[a1], 32), 32)]
            made.append(remote(
                src, dst, self.send.at[self.index, phase, d], self.recv.at[self.index, phase, d], peer
            ))
        return made

    def step(self, phase):
        blocks, at = pl.ds(self.first, self.count), self.place.at
        a1, a2, _ = self.axes
        if phase > 0:
            for copy in self.copies(phase - 1):
                copy.wait_recv()
        if phase == 1:
            mine = self.part[blocks, pl.ds(times(at[a1], 32), 32)]
            self.sum1[blocks] = (mine + self.recv1[0, blocks]) + (self.recv1[1, blocks] + self.recv1[2, blocks])
        elif phase == 2:
            mine = self.sum1[blocks, pl.ds(times(at[a2], 8), 8)]
            self.sum2[blocks] = (mine + self.recv2[0, blocks]) + (self.recv2[1, blocks] + self.recv2[2, blocks])
        elif phase == 3:
            fine = pl.ds(pl.multiple_of(at[a1] * 32 + at[a2] * 8, 8), 8)
            self.full[blocks, fine] = (self.sum2[blocks] + self.recv3[0, blocks]) + (
                self.recv3[1, blocks] + self.recv3[2, blocks]
            )
        if phase < 5:
            for copy in self.copies(phase):
                copy.start()

    def close(self):
        for phase in range(5):
            for copy in self.copies(phase):
                copy.wait_send()


def transposed_dot(left, right):
    return lax.dot_general(left, right, (((0,), (0,)), ((), ())), preferred_element_type=F32)


def thirds(value):
    high = value.astype(BF16)
    rest = value - high.astype(F32)
    middle = rest.astype(BF16)
    return high, middle, (rest - middle.astype(F32)).astype(BF16)


def panel_inverse(panels, lane0):
    sub = lax.broadcasted_iota(jnp.int32, (8, 128), 0)
    lane = lax.broadcasted_iota(jnp.int32, (8, 128), 1)
    pick = [sub == k for k in range(8)]
    for j in range(4):
        first = lane0 + 8 * j
        own = (lane >= first) & (lane < first + 8)
        eye = (lane - first == sub).astype(F32)
        for rows in panels:
            r = rows[j]
            cols = [jnp.broadcast_to(r[0][:, first + k:first + k + 1], (8, 128)) for k in range(8)]
            r = [jnp.where(own, eye, r[0])] + r[1:]
            for k in range(0, 8, 2):
                c0, c1 = cols[k], cols[k + 1]
                p, o, u, w = c0[k:k + 1, :], c1[k:k + 1, :], c0[k + 1:k + 2, :], c1[k + 1:k + 2, :]
                inv = 1.0 / (p * w - o * u)
                c0 = jnp.where(pick[k], -1.0, jnp.where(pick[k + 1], 0.0, c0))
                c1 = jnp.where(pick[k], 0.0, jnp.where(pick[k + 1], -1.0, c1))
                f0 = (c0 * w - c1 * u) * inv
                f1 = (c1 * p - c0 * o) * inv
                both = pick[k] | pick[k + 1]
                for n in range(k + 2, 8):
                    v = cols[n]
                    cols[n] = (jnp.where(both, 0.0, v) - f0 * v[k:k + 1, :]) - f1 * v[k + 1:k + 2, :]
                r = [(jnp.where(both, 0.0, v) - f0 * v[k:k + 1, :]) - f1 * v[k + 1:k + 2, :] for v in r]
            rows[j] = r
            for t in range(1, 4):
                i = (j + t) % 4
                c = rows[i][0]
                acc = [jnp.where(own, 0.0, c)] + rows[i][1:]
                for k in range(8):
                    wide = jnp.broadcast_to(c[:, first + k:first + k + 1], (8, 128))
                    acc = [v - wide * p[k:k + 1, :] for v, p in zip(acc, r)]
                rows[i] = acc
    return panels


def inverses(m, ahead, lefts, rights, beside, many=2):
    row = lax.broadcasted_iota(jnp.int32, (128, 128), 0)
    lane = lax.broadcasted_iota(jnp.int32, (128, 128), 1)
    short = lane[:32]

    def change(b, tile, q, left, right, live):
        lane0 = 32 * q
        mine = (lane >= lane0) & (lane < lane0 + 32) & live
        keep = mine & ((row < lane0) | (row >= lane0 + 32))
        for i in range(4):
            moved = jnp.dot(left[i], right, preferred_element_type=F32)
            for t in range(4):
                value = m[b, tile[i], tile[t]]
                if t == 0:
                    value = jnp.where(keep if i == 0 else mine, 0.0, value)
                m[b, tile[i], tile[t]] = value - moved[:, t * 128:(t + 1) * 128]

    def step(k, carry):
        beside(k)
        tile = [lax.rem(k + t, 4) for t in range(4)]
        before = [lax.rem(k + 3 + t, 4) for t in range(4)]
        waiting = [(before, 3, [lefts[b, i] for i in range(4)], rights[b], k > 0) for b in range(many)]
        old = [[ahead[b, t] for t in range(4)] for b in range(many)]
        for q in range(4):
            lane0 = 32 * q
            rows = pl.ds(lane0, 32)
            panels = panel_inverse([[[v[8 * i:8 * i + 8] for v in o] for i in range(4)] for o in old], lane0)
            following = []
            for b in range(many):
                change(b, *waiting[b])
                new = [jnp.concatenate([panels[b][i][t] for i in range(4)], axis=0) for t in range(4)]
                for t in range(4):
                    m[b, k, tile[t], rows, :] = new[t]
                left = [jnp.where(short < lane0, -old[b][0], jnp.where(short < lane0 + 32, 0.0, old[b][0]))]
                left += [old[b][t] * jnp.where(k + t >= 4, -1.0, 1.0) for t in range(1, 4)]
                rh, rm, rl = thirds(jnp.concatenate(new, axis=1))
                right = jnp.concatenate([rh, rm, rh, rl, rm, rh], axis=0)
                turned = []
                for i in range(4):
                    lh, lm, ll = thirds(left[i])
                    turned.append(jnp.concatenate([lh, lh, lm, lh, lm, ll], axis=0).T)
                waiting[b] = (tile, q, turned, right, True)
                if q < 3:
                    some, block, turn = pl.ds(lane0 + 32, 32), k, turned[0][lane0 + 32:lane0 + 64]
                else:
                    some, block, turn = pl.ds(0, 32), tile[1], turned[1][:32]
                moved = jnp.dot(turn, right, preferred_element_type=F32)
                mine = (short >= lane0) & (short < lane0 + 32)
                nxt = []
                for t in range(4):
                    value = m[b, block, tile[t], some, :]
                    if t == 0:
                        value = jnp.where(mine, 0.0, value)
                    nxt.append(value - moved[:, t * 128:(t + 1) * 128])
                following.append(nxt)
            old = following
        for b in range(many):
            for t in range(4):
                ahead[b, t] = old[b][(t + 1) % 4]
                lefts[b, t] = waiting[b][2][t]
            rights[b] = waiting[b][3]
        return carry

    for b in range(many):
        for t in range(4):
            ahead[b, t] = m[b, 0, t, 0:32, :]
            lefts[b, t] = jnp.zeros((128, 192), BF16)
        rights[b] = jnp.zeros((192, 512), BF16)
    lax.fori_loop(0, 4, step, 0)
    for b in range(many):
        change(b, [3, 0, 1, 2], 3, [lefts[b, i] for i in range(4)], rights[b], True)


def spread(full, first, m, b, scale, column):
    row = lax.broadcasted_iota(jnp.int32, (128, 128), 0)
    lane = lax.broadcasted_iota(jnp.int32, (128, 128), 1)
    down = []
    for i in range(4):
        block = full[first + PAIRS.index((i, i))]
        diagonal = jnp.where(row == lane, block + damping_level, 0.0)
        scale[b, i] = lax.rsqrt(jnp.broadcast_to(jnp.sum(diagonal, axis=0, keepdims=True), (8, 128)))
        down.append(lax.rsqrt(jnp.broadcast_to(jnp.sum(diagonal, axis=1, keepdims=True), (128, 128))))
        if column is not None:
            column[i] = down[i]
    for t, (i, j) in enumerate(PAIRS):
        block = full[first + t]
        if i == j:
            block = jnp.where(row == lane, block + damping_level, block)
        block = (block * down[i]) * scale[b, j, 0:1, :]
        m[b, i, j] = block
        if i != j:
            m[b, j, i] = block.T


def finish(m, full, scale, column, row, out_ref):
    rows = pl.ds(pl.multiple_of(lax.rem(row, 128), 8), 8)
    block = lax.div(row, 128)
    total = None
    for i in range(4):
        left = (m[0, block, i, rows, :] * column[block, rows, :]) * scale[0, i]
        wide = jnp.concatenate([full[20 + i * 4 + j] for j in range(4)], axis=1)
        part = jnp.dot(left, wide, precision=HIGHEST, preferred_element_type=F32)
        total = part if total is None else total + part
    out = None
    for i in range(4):
        wide = jnp.concatenate([m[1, i, j] for j in range(4)], axis=1)
        left = total[:, i * 128:(i + 1) * 128] * scale[1, i]
        part = jnp.dot(left, wide, precision=HIGHEST, preferred_element_type=F32)
        out = part if out is None else out + part
    for j in range(4):
        out_ref[:, j * 128:(j + 1) * 128] = out[:, j * 128:(j + 1) * 128] * scale[1, j]


def kernel(x_hbm, w_hbm, top_hbm, out_ref, weights, kept, slopes, grads, top, part, full,
           recv1, sum1, recv2, sum2, recv3, m, ahead, lefts, rights, scale, column,
           gather_send, gather_recv, sum_send, sum_recv, local):
    place = Place()
    loads = [
        pltpu.make_async_copy(w_hbm, weights.at[place.core, 0], local.at[0]),
        pltpu.make_async_copy(x_hbm, kept.at[0], local.at[1]),
        pltpu.make_async_copy(top_hbm, top, local.at[2]),
    ]
    for load in loads:
        load.start()
    enter(place)
    gather = Gather(place, w_hbm, weights, gather_send, gather_recv)
    gather.run()
    for load in loads:
        load.wait()

    def weight_of(layer):
        return weights.at[lax.rem(layer, 2), lax.rem(lax.div(layer, 2) - place.high + 4, 4)]

    def forward(layer, carry):
        x = kept[layer]
        z = jnp.dot(x, weight_of(layer)[...], preferred_element_type=F32)
        squared = z * z
        tangent = jnp.tanh(gelu_coef * (z + cubic_coef * squared * z))
        slopes[layer] = 0.5 * (1.0 + tangent) + 0.5 * z * (1.0 - tangent * tangent) * gelu_coef * (
            1.0 + 3.0 * cubic_coef * squared
        )
        kept[layer + 1] = (x.astype(F32) + 0.5 * z * (1.0 + tangent)).astype(BF16)
        return carry

    lax.fori_loop(0, 8, forward, 0)

    bufs = (recv1, sum1, recv2, sum2, recv3)
    make = lambda groups, base: [
        Sum(place, g, base + n, part, full, bufs, sum_send, sum_recv) for n, g in enumerate(groups)
    ]
    acts, gradsums, weightsums = make(ACT_GROUPS, 0), make(GRAD_GROUPS, 2), make(WEIGHT_GROUPS, 4)

    def step(groups, phase):
        for group in groups:
            group.step(phase)

    x = kept[place.section]
    for i in range(4):
        product = transposed_dot(x[:, i * 128:(i + 1) * 128], x[:, i * 128:]) * (1.0 / 8192.0)
        for j in range(i, 4):
            part[PAIRS.index((i, j))] = product[:, (j - i) * 128:(j - i + 1) * 128]
    step(acts, 0)

    def backward(number, upstream):
        layer = 7 - number
        grad = (upstream.astype(F32) * slopes[layer]).astype(BF16)
        grads[layer] = grad
        return (
            upstream.astype(F32)
            + lax.dot_general(grad, weight_of(layer)[...], (((1,), (1,)), ((), ())), preferred_element_type=F32)
        ).astype(BF16)

    upstream = (top[...].astype(F32) * loss_scale).astype(BF16)
    lax.fori_loop(0, 8, backward, upstream)
    g = grads[place.section]
    for i in range(4):
        product = transposed_dot(g[:, i * 128:(i + 1) * 128], g[:, i * 128:])
        for j in range(i, 4):
            part[10 + PAIRS.index((i, j))] = product[:, (j - i) * 128:(j - i + 1) * 128]
    step(gradsums, 0)
    step(acts, 1)
    for i in range(4):
        product = transposed_dot(x[:, i * 128:(i + 1) * 128], g)
        for j in range(4):
            part[20 + 4 * i + j] = product[:, j * 128:(j + 1) * 128]
    step(acts, 2)
    step(gradsums, 1)
    step(acts, 3)
    step(gradsums, 2)
    step(weightsums, 0)
    step(acts, 4)
    step(gradsums, 3)
    step(acts, 5)
    spread(full, 0, m, 0, scale, column)
    step(gradsums, 4)
    step(weightsums, 1)
    step(gradsums, 5)
    spread(full, 10, m, 1, scale, None)

    def beside(k):
        for number in range(1, 4):
            pl.when(k == number)(functools.partial(step, weightsums, number + 1))

    inverses(m, ahead, lefts, rights, beside)
    step(weightsums, 5)
    finish(m, full, scale, column, place.dp * 8, out_ref)
    gather.close()
    for group in acts + gradsums + weightsums:
        group.close()


def preconditioned(x, w, top):
    return pl.pallas_call(
        kernel,
        out_shape=jax.ShapeDtypeStruct((8, 512), F32),
        in_specs=[pl.BlockSpec(memory_space=pltpu.HBM)] * 3,
        out_specs=pl.BlockSpec(memory_space=pltpu.VMEM),
        scratch_shapes=[
            pltpu.VMEM((2, 4, 512, 512), BF16),
            pltpu.VMEM((9, 128, 512), BF16),
            pltpu.VMEM((8, 128, 512), F32),
            pltpu.VMEM((8, 128, 512), BF16),
            pltpu.VMEM((128, 512), BF16),
            pltpu.VMEM((36, 128, 128), F32),
            pltpu.VMEM((36, 128, 128), F32),
            pltpu.VMEM((3, 36, 32, 128), F32),
            pltpu.VMEM((36, 32, 128), F32),
            pltpu.VMEM((3, 36, 8, 128), F32),
            pltpu.VMEM((36, 8, 128), F32),
            pltpu.VMEM((3, 36, 8, 128), F32),
            pltpu.VMEM((2, 4, 4, 128, 128), F32),
            pltpu.VMEM((2, 4, 32, 128), F32),
            pltpu.VMEM((2, 4, 128, 192), BF16),
            pltpu.VMEM((2, 192, 512), BF16),
            pltpu.VMEM((2, 4, 8, 128), F32),
            pltpu.VMEM((4, 128, 128), F32),
            pltpu.SemaphoreType.DMA((40,)),
            pltpu.SemaphoreType.DMA((40,)),
            pltpu.SemaphoreType.DMA((6, 5, 3)),
            pltpu.SemaphoreType.DMA((6, 5, 3)),
            pltpu.SemaphoreType.DMA((3,)),
        ],
        compiler_params=pltpu.CompilerParams(
            collective_id=0, has_side_effects=True, vmem_limit_bytes=40 << 20
        ),
    )(x, w, top)


def body(inputs, weights, cotangent):
    rows = preconditioned(inputs.reshape(128, 512), weights[0, 0], cotangent.reshape(128, 512))
    return rows[None, None]


def solution(mesh):
    placed = (P(None, "dp", None), P("section", None, None, None), P(None, "dp", None))
    return jax.shard_map(
        body, mesh=mesh, in_specs=placed, out_specs=P("section", None, "dp", None), check_vma=False
    )
```

time: 1650 us -> 109 us (0.07)
  the two profiles are of different devices: /device:TPU:32 before, /device:TPU:1 now
where the time goes in v1:
time: 109 us; the launch traced here: 108 us
  Pallas kernels  104 us (95%)
  local copies, waits for them, and re-layouts  3.46 us (3%)
    pallas_call x1, Pallas kernels, preconditioned(): pl.pallas_call(kernel, out_shape=jax.ShapeDtypeStruct((8, 512), F32), in_...  104 us
    unnamed x7, local copies, waits for them, and re-layouts  3.46 us

profile of v1, /device:TPU:1, one launch (start us, length us, event | category | flops | bytes accessed | tf_op | source)
XLA Modules:
  0.0 107.7 jit_solution(17148779467237591796)
XLA Ops:
  0.0 0.0 copy-start
  0.0 1.0 copy-done
  1.0 0.0 copy-start.1
  1.0 0.9 copy-done.1
  1.9 0.0 copy-start.2
  1.9 0.9 copy-done.2
  2.9 104.2 %shard_map.37 = f32[8,512]{1,0:T(8,128)S(1)} custom-call(bf16[128,512]{1,0:T(8,128)(2,1)S(1)} %bitcast.5, bf16[512,512]{1,0:T(8,128)(2,1)S(1)} %bitcast.4, bf16[128,512]{1,0:T(8,128)(2,1)S(1)} %bitcast.6), custom_call_target="tpu_custom_call" | custom-call | tf_op jit(solution)/shard_map/pallas_call | solution.py:434
  107.1 0.6 copy.5
Async XLA Ops:
  0.0 1.0 copy-start
  1.0 0.9 copy-start.1
  1.9 0.9 copy-start.2

commit v2 on v1

--- a/solution.py
+++ b/solution.py
@@ -406,21 +406,22 @@
             part[20 + 4 * i + j] = product[:, j * 128:(j + 1) * 128]
     step(acts, 2)
     step(gradsums, 1)
+    step(weightsums, 0)
     step(acts, 3)
     step(gradsums, 2)
-    step(weightsums, 0)
     step(acts, 4)
     step(gradsums, 3)
+    step(weightsums, 1)
     step(acts, 5)
     spread(full, 0, m, 0, scale, column)
     step(gradsums, 4)
-    step(weightsums, 1)
+    step(weightsums, 2)
     step(gradsums, 5)
     spread(full, 10, m, 1, scale, None)
 
     def beside(k):
-        for number in range(1, 4):
-            pl.when(k == number)(functools.partial(step, weightsums, number + 1))
+        for number in range(1, 3):
+            pl.when(k == number)(functools.partial(step, weightsums, number + 2))
 
     inverses(m, ahead, lefts, rights, beside)
     step(weightsums, 5)

time: 109 us -> 105 us (0.963)
  Pallas kernels: 104 us -> 101 us
    pallas_call x1, Pallas kernels: 104 us -> 101 us  [preconditioned(): pl.pallas_call(kernel, out_shape=jax.ShapeDtypeStruct((8, 512), F32), in_...]
where the time goes in v2:
time: 105 us; the launch traced here: 104 us
  Pallas kernels  101 us (96%)
  local copies, waits for them, and re-layouts  3.46 us (3%)
    pallas_call x1, Pallas kernels, preconditioned(): pl.pallas_call(kernel, out_shape=jax.ShapeDtypeStruct((8, 512), F32), in_...  101 us
    unnamed x7, local copies, waits for them, and re-layouts  3.46 us

profile of v2, /device:TPU:1, one launch (start us, length us, event | category | flops | bytes accessed | tf_op | source)
XLA Modules:
  0.0 104.0 jit_solution(15312969764583787560)
XLA Ops:
  0.0 0.0 copy-start
  0.0 1.0 copy-done
  1.0 0.0 copy-start.1
  1.0 0.9 copy-done.1
  1.9 0.0 copy-start.2
  1.9 0.9 copy-done.2
  2.9 100.5 %shard_map.37 = f32[8,512]{1,0:T(8,128)S(1)} custom-call(bf16[128,512]{1,0:T(8,128)(2,1)S(1)} %bitcast.5, bf16[512,512]{1,0:T(8,128)(2,1)S(1)} %bitcast.4, bf16[128,512]{1,0:T(8,128)(2,1)S(1)} %bitcast.6), custom_call_target="tpu_custom_call" | custom-call | tf_op jit(solution)/shard_map/pallas_call | solution.py:435
  103.4 0.6 copy.5
Async XLA Ops:
  0.0 1.0 %copy-start = (bf16[1,1,512,512]{3,2,1,0:T(8,128)(2,1)S(1)}, bf16[1,1,512,512]{3,2,1,0:T(8,128)(2,1)}, u32[]{:S(2)}) copy-start(bf16[1,1,512,512]{3,2,1,0:T(8,128)(2,1)} %param.4) | copy-start | bytes 1572868
  1.0 0.9 copy-start.1
  1.9 0.9 copy-start.2

commit v3 on v2

--- a/solution.py
+++ b/solution.py
@@ -43,8 +43,8 @@
 
 def enter(place):
     barrier = pltpu.get_barrier_semaphore()
-    peers = [place.sibling()] + [place.other_high(t) for t in range(1, 4)]
-    peers += [place.along(a, t)[1] for a in "yxz" for t in range(1, 4)]
+    peers = [place.other_high(t) for t in (2, 1, 3)]
+    peers += [place.along(a, t)[1] for a in "zyx" for t in (2, 1, 3)] + [place.sibling()]
     for peer in peers:
         pl.semaphore_signal(barrier, inc=1, device_id=peer, device_id_type=MESH)
     pl.semaphore_wait(barrier, len(peers))
@@ -78,34 +78,36 @@
         return copy
 
     def run(self):
-        place, full = self.place, self.full
-        mine = full.at[place.core]
-        pending = [[], []]
-        for t in (1, 3, 2):
+        place, mine = self.place, self.full.at[self.place.core]
+        numbers = iter(range(64))
+        arrivals = {}
+        for slot, t in ((1, 1), (2, 3), (3, 2)):
             for half in range(2):
                 part = (self.rows(half, False), pl.ds(half * 256, 256))
-                pending[half].append(self.go(
-                    6 * half + t - 1, self.own.at[part], mine.at[(t, *part)], place.other_high(4 - t)
+                arrivals.setdefault((slot // 3, half), []).append(self.go(
+                    next(numbers), self.own.at[part], mine.at[(slot, *part)], place.other_high(4 - t)
                 ))
-        swaps = [self.go(31, self.own, mine.at[0], place.sibling())]
+        swaps = [self.go(next(numbers), self.own, mine.at[0], place.sibling())]
+        slots = [pl.ds(1, 2), pl.ds(3, 1)]
         for phase in range(2):
-            for half in range(2):
-                for copy in pending[half]:
-                    copy.wait_recv()
-                block = mine.at[pl.ds(1, 3), self.rows(half, phase == 1), pl.ds(half * 256, 256)]
-                axis = GATHER_AXES[half][1 - phase]
-                pending[half] = [
-                    self.go(6 * half + (3 if phase == 0 else 12) + d - 1, block, block, place.along(axis, d)[1])
-                    for d in (1, 3, 2)
-                ]
-                if phase == 1:
-                    swaps.append(self.go(24 + half, block, block, place.sibling()))
-        for number, d in enumerate((1, 3, 2)):
-            for half in range(2):
-                pending[half][number].wait_recv()
-                origin = lax.rem(place.at[GATHER_AXES[half][0]] + 4 - d, 4)
-                block = mine.at[pl.ds(1, 3), pl.ds(times(origin, 128), 128), pl.ds(half * 256, 256)]
-                swaps.append(self.go(26 + half + 6 + 2 * number, block, block, place.sibling()))
+            for chunk in range(2):
+                for half in range(2):
+                    for copy in arrivals[chunk, half]:
+                        copy.wait_recv()
+                    block = mine.at[slots[chunk], self.rows(half, phase == 1), pl.ds(half * 256, 256)]
+                    axis = GATHER_AXES[half][1 - phase]
+                    arrivals[chunk, half] = [
+                        self.go(next(numbers), block, block, place.along(axis, d)[1]) for d in (1, 3, 2)
+                    ]
+                    if phase == 1:
+                        swaps.append(self.go(next(numbers), block, block, place.sibling()))
+        for chunk in range(2):
+            for number, d in enumerate((1, 3, 2)):
+                for half in range(2):
+                    arrivals[chunk, half][number].wait_recv()
+                    origin = lax.rem(place.at[GATHER_AXES[half][0]] + 4 - d, 4)
+                    block = mine.at[slots[chunk], pl.ds(times(origin, 128), 128), pl.ds(half * 256, 256)]
+                    swaps.append(self.go(next(numbers), block, block, place.sibling()))
         for copy in swaps:
             copy.wait_recv()
 
@@ -182,7 +184,7 @@
     return high, middle, (rest - middle.astype(F32)).astype(BF16)
 
 
-def panel_inverse(panels, lane0):
+def panel_inverse(panels, lane0, between):
     sub = lax.broadcasted_iota(jnp.int32, (8, 128), 0)
     lane = lax.broadcasted_iota(jnp.int32, (8, 128), 1)
     pick = [sub == k for k in range(8)]
@@ -200,13 +202,12 @@
                 inv = 1.0 / (p * w - o * u)
                 c0 = jnp.where(pick[k], -1.0, jnp.where(pick[k + 1], 0.0, c0))
                 c1 = jnp.where(pick[k], 0.0, jnp.where(pick[k + 1], -1.0, c1))
-                f0 = (c0 * w - c1 * u) * inv
-                f1 = (c1 * p - c0 * o) * inv
-                both = pick[k] | pick[k + 1]
+                f0 = (c0 * w - c1 * u) * inv + jnp.where(pick[k], 1.0, 0.0)
+                f1 = (c1 * p - c0 * o) * inv + jnp.where(pick[k + 1], 1.0, 0.0)
                 for n in range(k + 2, 8):
                     v = cols[n]
-                    cols[n] = (jnp.where(both, 0.0, v) - f0 * v[k:k + 1, :]) - f1 * v[k + 1:k + 2, :]
-                r = [(jnp.where(both, 0.0, v) - f0 * v[k:k + 1, :]) - f1 * v[k + 1:k + 2, :] for v in r]
+                    cols[n] = (v - f0 * v[k:k + 1, :]) - f1 * v[k + 1:k + 2, :]
+                r = [(v - f0 * v[k:k + 1, :]) - f1 * v[k + 1:k + 2, :] for v in r]
             rows[j] = r
             for t in range(1, 4):
                 i = (j + t) % 4
@@ -216,6 +217,7 @@
                     wide = jnp.broadcast_to(c[:, first + k:first + k + 1], (8, 128))
                     acc = [v - wide * p[k:k + 1, :] for v, p in zip(acc, r)]
                 rows[i] = acc
+        between(j)
     return panels
 
 
@@ -224,11 +226,11 @@
     lane = lax.broadcasted_iota(jnp.int32, (128, 128), 1)
     short = lane[:32]
 
-    def change(b, tile, q, left, right, live):
+    def change(b, blocks, tile, q, left, right, live):
         lane0 = 32 * q
         mine = (lane >= lane0) & (lane < lane0 + 32) & live
         keep = mine & ((row < lane0) | (row >= lane0 + 32))
-        for i in range(4):
+        for i in blocks:
             moved = jnp.dot(left[i], right, preferred_element_type=F32)
             for t in range(4):
                 value = m[b, tile[i], tile[t]]
@@ -245,10 +247,9 @@
         for q in range(4):
             lane0 = 32 * q
             rows = pl.ds(lane0, 32)
-            panels = panel_inverse([[[v[8 * i:8 * i + 8] for v in o] for i in range(4)] for o in old], lane0)
+            panels = panel_inverse([[[v[8 * i:8 * i + 8] for v in o] for i in range(4)] for o in old], lane0, lambda j: [change(b, [j], *waiting[b]) for b in range(many)])
             following = []
             for b in range(many):
-                change(b, *waiting[b])
                 new = [jnp.concatenate([panels[b][i][t] for i in range(4)], axis=0) for t in range(4)]
                 for t in range(4):
                     m[b, k, tile[t], rows, :] = new[t]
@@ -289,7 +290,7 @@
         rights[b] = jnp.zeros((192, 512), BF16)
     lax.fori_loop(0, 4, step, 0)
     for b in range(many):
-        change(b, [3, 0, 1, 2], 3, [lefts[b, i] for i in range(4)], rights[b], True)
+        change(b, range(4), [3, 0, 1, 2], 3, [lefts[b, i] for i in range(4)], rights[b], True)
 
 
 def spread(full, first, m, b, scale, column):
@@ -350,7 +351,8 @@
         load.wait()
 
     def weight_of(layer):
-        return weights.at[lax.rem(layer, 2), lax.rem(lax.div(layer, 2) - place.high + 4, 4)]
+        t = lax.rem(lax.div(layer, 2) - place.high + 4, 4)
+        return weights.at[lax.rem(layer, 2), t + lax.div(t, 2) - 2 * lax.div(t, 3)]
 
     def forward(layer, carry):
         x = kept[layer]
@@ -404,17 +406,17 @@
         product = transposed_dot(x[:, i * 128:(i + 1) * 128], g)
         for j in range(4):
             part[20 + 4 * i + j] = product[:, j * 128:(j + 1) * 128]
+    step(gradsums, 1)
     step(acts, 2)
-    step(gradsums, 1)
     step(weightsums, 0)
+    step(gradsums, 2)
     step(acts, 3)
-    step(gradsums, 2)
+    step(gradsums, 3)
     step(acts, 4)
-    step(gradsums, 3)
     step(weightsums, 1)
+    step(gradsums, 4)
     step(acts, 5)
     spread(full, 0, m, 0, scale, column)
-    step(gradsums, 4)
     step(weightsums, 2)
     step(gradsums, 5)
     spread(full, 10, m, 1, scale, None)
@@ -456,8 +458,8 @@
             pltpu.VMEM((2, 192, 512), BF16),
             pltpu.VMEM((2, 4, 8, 128), F32),
             pltpu.VMEM((4, 128, 128), F32),
-            pltpu.SemaphoreType.DMA((40,)),
-            pltpu.SemaphoreType.DMA((40,)),
+            pltpu.SemaphoreType.DMA((64,)),
+            pltpu.SemaphoreType.DMA((64,)),
             pltpu.SemaphoreType.DMA((6, 5, 3)),
             pltpu.SemaphoreType.DMA((6, 5, 3)),
             pltpu.SemaphoreType.DMA((3,)),

time: 105 us -> 102 us (0.971)
  Pallas kernels: 101 us -> 98.4 us
    pallas_call x1, Pallas kernels: 101 us -> 98.4 us  [preconditioned(): pl.pallas_call(kernel, out_shape=jax.ShapeDtypeStruct((8, 512), F32), in_...]
where the time goes in v3:
time: 102 us
  Pallas kernels  98.4 us (96%)
  local copies, waits for them, and re-layouts  3.46 us (3%)
    pallas_call x1, Pallas kernels, preconditioned(): pl.pallas_call(kernel, out_shape=jax.ShapeDtypeStruct((8, 512), F32), in_...  98.4 us
    unnamed x7, local copies, waits for them, and re-layouts  3.46 us

profile of v3, /device:TPU:1, one launch (start us, length us, event | category | flops | bytes accessed | tf_op | source)
XLA Modules:
  0.0 101.8 jit_solution(4490308740538686855)
XLA Ops:
  0.0 0.0 copy-start
  0.0 1.0 %copy-done = bf16[1,1,512,512]{3,2,1,0:T(8,128)(2,1)S(1)} copy-done((bf16[1,1,512,512]{3,2,1,0:T(8,128)(2,1)S(1)}, bf16[1,1,512,512]{3,2,1,0:T(8,128)(2,1)}, u32[]{:S(2)}) %copy-start) | copy-done | bytes 524312
  1.0 0.0 copy-start.1
  1.0 0.9 copy-done.1
  1.9 0.0 copy-start.2
  1.9 0.9 copy-done.2
  2.9 98.4 %shard_map.37 = f32[8,512]{1,0:T(8,128)S(1)} custom-call(bf16[128,512]{1,0:T(8,128)(2,1)S(1)} %bitcast.5, bf16[512,512]{1,0:T(8,128)(2,1)S(1)} %bitcast.4, bf16[128,512]{1,0:T(8,128)(2,1)S(1)} %bitcast.6), custom_call_target="tpu_custom_call" | custom-call | tf_op jit(solution)/shard_map/pallas_call | solution.py:437
  101.2 0.6 copy.5
Async XLA Ops:
  0.0 1.0 %copy-start = (bf16[1,1,512,512]{3,2,1,0:T(8,128)(2,1)S(1)}, bf16[1,1,512,512]{3,2,1,0:T(8,128)(2,1)}, u32[]{:S(2)}) copy-start(bf16[1,1,512,512]{3,2,1,0:T(8,128)(2,1)} %param.4) | copy-start | bytes 1572868
  1.0 0.9 copy-start.1
  1.9 0.9 copy-start.2

commit v4 on v3

--- a/solution.py
+++ b/solution.py
@@ -77,7 +77,7 @@
         self.sent.append(copy)
         return copy
 
-    def run(self):
+    def run(self, beside):
         place, mine = self.place, self.full.at[self.place.core]
         numbers = iter(range(64))
         arrivals = {}
@@ -87,7 +87,9 @@
                 arrivals.setdefault((slot // 3, half), []).append(self.go(
                     next(numbers), self.own.at[part], mine.at[(slot, *part)], place.other_high(4 - t)
                 ))
-        swaps = [self.go(next(numbers), self.own, mine.at[0], place.sibling())]
+        self.go(next(numbers), self.own, mine.at[0], place.sibling()).wait_recv()
+        swaps = []
+        beside(0)
         slots = [pl.ds(1, 2), pl.ds(3, 1)]
         for phase in range(2):
             for chunk in range(2):
@@ -101,6 +103,7 @@
                     ]
                     if phase == 1:
                         swaps.append(self.go(next(numbers), block, block, place.sibling()))
+            beside(1 + phase)
         for chunk in range(2):
             for number, d in enumerate((1, 3, 2)):
                 for half in range(2):
@@ -221,7 +224,7 @@
     return panels
 
 
-def inverses(m, ahead, lefts, rights, beside, many=2):
+def inverses(m, ahead, lefts, rights, beside, first, many):
     row = lax.broadcasted_iota(jnp.int32, (128, 128), 0)
     lane = lax.broadcasted_iota(jnp.int32, (128, 128), 1)
     short = lane[:32]
@@ -233,17 +236,17 @@
         for i in blocks:
             moved = jnp.dot(left[i], right, preferred_element_type=F32)
             for t in range(4):
-                value = m[b, tile[i], tile[t]]
+                value = m[first + b, tile[i], tile[t]]
                 if t == 0:
                     value = jnp.where(keep if i == 0 else mine, 0.0, value)
-                m[b, tile[i], tile[t]] = value - moved[:, t * 128:(t + 1) * 128]
+                m[first + b, tile[i], tile[t]] = value - moved[:, t * 128:(t + 1) * 128]
 
     def step(k, carry):
         beside(k)
         tile = [lax.rem(k + t, 4) for t in range(4)]
         before = [lax.rem(k + 3 + t, 4) for t in range(4)]
-        waiting = [(before, 3, [lefts[b, i] for i in range(4)], rights[b], k > 0) for b in range(many)]
-        old = [[ahead[b, t] for t in range(4)] for b in range(many)]
+        waiting = [(before, 3, [lefts[first + b, i] for i in range(4)], rights[first + b], k > 0) for b in range(many)]
+        old = [[ahead[first + b, t] for t in range(4)] for b in range(many)]
         for q in range(4):
             lane0 = 32 * q
             rows = pl.ds(lane0, 32)
@@ -252,7 +255,7 @@
             for b in range(many):
                 new = [jnp.concatenate([panels[b][i][t] for i in range(4)], axis=0) for t in range(4)]
                 for t in range(4):
-                    m[b, k, tile[t], rows, :] = new[t]
+                    m[first + b, k, tile[t], rows, :] = new[t]
                 left = [jnp.where(short < lane0, -old[b][0], jnp.where(short < lane0 + 32, 0.0, old[b][0]))]
                 left += [old[b][t] * jnp.where(k + t >= 4, -1.0, 1.0) for t in range(1, 4)]
                 rh, rm, rl = thirds(jnp.concatenate(new, axis=1))
@@ -270,7 +273,7 @@
                 mine = (short >= lane0) & (short < lane0 + 32)
                 nxt = []
                 for t in range(4):
-                    value = m[b, block, tile[t], some, :]
+                    value = m[first + b, block, tile[t], some, :]
                     if t == 0:
                         value = jnp.where(mine, 0.0, value)
                     nxt.append(value - moved[:, t * 128:(t + 1) * 128])
@@ -278,19 +281,19 @@
             old = following
         for b in range(many):
             for t in range(4):
-                ahead[b, t] = old[b][(t + 1) % 4]
-                lefts[b, t] = waiting[b][2][t]
-            rights[b] = waiting[b][3]
+                ahead[first + b, t] = old[b][(t + 1) % 4]
+                lefts[first + b, t] = waiting[b][2][t]
+            rights[first + b] = waiting[b][3]
         return carry
 
     for b in range(many):
         for t in range(4):
-            ahead[b, t] = m[b, 0, t, 0:32, :]
-            lefts[b, t] = jnp.zeros((128, 192), BF16)
-        rights[b] = jnp.zeros((192, 512), BF16)
+            ahead[first + b, t] = m[first + b, 0, t, 0:32, :]
+            lefts[first + b, t] = jnp.zeros((128, 192), BF16)
+        rights[first + b] = jnp.zeros((192, 512), BF16)
     lax.fori_loop(0, 4, step, 0)
     for b in range(many):
-        change(b, range(4), [3, 0, 1, 2], 3, [lefts[b, i] for i in range(4)], rights[b], True)
+        change(b, range(4), [3, 0, 1, 2], 3, [lefts[first + b, i] for i in range(4)], rights[first + b], True)
 
 
 def spread(full, first, m, b, scale, column):
@@ -345,11 +348,6 @@
     for load in loads:
         load.start()
     enter(place)
-    gather = Gather(place, w_hbm, weights, gather_send, gather_recv)
-    gather.run()
-    for load in loads:
-        load.wait()
-
     def weight_of(layer):
         t = lax.rem(lax.div(layer, 2) - place.high + 4, 4)
         return weights.at[lax.rem(layer, 2), t + lax.div(t, 2) - 2 * lax.div(t, 3)]
@@ -365,8 +363,6 @@
         kept[layer + 1] = (x.astype(F32) + 0.5 * z * (1.0 + tangent)).astype(BF16)
         return carry
 
-    lax.fori_loop(0, 8, forward, 0)
-
     bufs = (recv1, sum1, recv2, sum2, recv3)
     make = lambda groups, base: [
         Sum(place, g, base + n, part, full, bufs, sum_send, sum_recv) for n, g in enumerate(groups)
@@ -377,12 +373,36 @@
         for group in groups:
             group.step(phase)
 
-    x = kept[place.section]
-    for i in range(4):
-        product = transposed_dot(x[:, i * 128:(i + 1) * 128], x[:, i * 128:]) * (1.0 / 8192.0)
-        for j in range(i, 4):
-            part[PAIRS.index((i, j))] = product[:, (j - i) * 128:(j - i + 1) * 128]
-    step(acts, 0)
+    def act_sum():
+        x = kept[place.section]
+        for i in range(4):
+            product = transposed_dot(x[:, i * 128:(i + 1) * 128], x[:, i * 128:]) * (1.0 / 8192.0)
+            for j in range(i, 4):
+                part[PAIRS.index((i, j))] = product[:, (j - i) * 128:(j - i + 1) * 128]
+        step(acts, 0)
+
+    early, late = pl.when(place.high == 0), pl.when(place.high != 0)
+
+    def ahead_of_layers(number):
+        if number == 0:
+            forward(0, 0)
+            act_sum()
+        else:
+            step(acts, number)
+
+    gather = Gather(place, w_hbm, weights, gather_send, gather_recv)
+
+    def beside_gather(number):
+        if number == 0:
+            for load in loads:
+                load.wait()
+        early(functools.partial(ahead_of_layers, number))
+
+    gather.run(beside_gather)
+    early(functools.partial(step, acts, 3))
+    lax.fori_loop(0, 8, forward, 0)
+    early(functools.partial(step, acts, 4))
+    late(act_sum)
 
     def backward(number, upstream):
         layer = 7 - number
@@ -401,31 +421,46 @@
         for j in range(i, 4):
             part[10 + PAIRS.index((i, j))] = product[:, (j - i) * 128:(j - i + 1) * 128]
     step(gradsums, 0)
-    step(acts, 1)
+    late(functools.partial(step, acts, 1))
+    x = kept[place.section]
     for i in range(4):
         product = transposed_dot(x[:, i * 128:(i + 1) * 128], g)
         for j in range(4):
             part[20 + 4 * i + j] = product[:, j * 128:(j + 1) * 128]
-    step(gradsums, 1)
-    step(acts, 2)
-    step(weightsums, 0)
-    step(gradsums, 2)
-    step(acts, 3)
-    step(gradsums, 3)
-    step(acts, 4)
-    step(weightsums, 1)
-    step(gradsums, 4)
-    step(acts, 5)
-    spread(full, 0, m, 0, scale, column)
-    step(weightsums, 2)
-    step(gradsums, 5)
-    spread(full, 10, m, 1, scale, None)
-
-    def beside(k):
-        for number in range(1, 3):
-            pl.when(k == number)(functools.partial(step, weightsums, number + 2))
-
-    inverses(m, ahead, lefts, rights, beside)
+
+    def in_order(*steps):
+        for groups, phase in steps:
+            step(groups, phase)
+
+    def at(table):
+        def beside(k):
+            for number, steps in table.items():
+                pl.when(k == number)(functools.partial(in_order, *steps))
+        return beside
+
+    inverse_refs = (m, ahead, lefts, rights)
+    last = at({1: [(weightsums, 3)], 2: [(weightsums, 4)]})
+
+    def one_by_one():
+        step(acts, 5)
+        spread(full, 0, m, 0, scale, column)
+        inverses(*inverse_refs, at({
+            1: [(gradsums, 1), (weightsums, 0)], 2: [(gradsums, 2)], 3: [(gradsums, 3), (weightsums, 1)],
+        }), 0, 1)
+        in_order((gradsums, 4), (weightsums, 2), (gradsums, 5))
+        spread(full, 10, m, 1, scale, None)
+        inverses(*inverse_refs, last, 1, 1)
+
+    def together():
+        in_order((gradsums, 1), (acts, 2), (weightsums, 0), (gradsums, 2), (acts, 3), (gradsums, 3), (acts, 4),
+                 (weightsums, 1), (gradsums, 4), (acts, 5))
+        spread(full, 0, m, 0, scale, column)
+        in_order((weightsums, 2), (gradsums, 5))
+        spread(full, 10, m, 1, scale, None)
+        inverses(*inverse_refs, last, 0, 2)
+
+    early(one_by_one)
+    late(together)
     step(weightsums, 5)
     finish(m, full, scale, column, place.dp * 8, out_ref)
     gather.close()

time: 102 us -> 99.1 us (0.972)
  Pallas kernels: 98.4 us -> 95 us
    pallas_call x1, Pallas kernels: 98.4 us -> 95 us  [preconditioned(): pl.pallas_call(kernel, out_shape=jax.ShapeDtypeStruct((8, 512), F32), in_...]
where the time goes in v4:
time: 99.1 us; the launch traced here: 98.5 us
  Pallas kernels  95 us (96%)
  local copies, waits for them, and re-layouts  3.46 us (3%)
    pallas_call x1, Pallas kernels, preconditioned(): pl.pallas_call(kernel, out_shape=jax.ShapeDtypeStruct((8, 512), F32), in_...  95 us
    unnamed x7, local copies, waits for them, and re-layouts  3.46 us

profile of v4, /device:TPU:1, one launch (start us, length us, event | category | flops | bytes accessed | tf_op | source)
XLA Modules:
  0.0 98.5 jit_solution(9215988859594022635)
XLA Ops:
  0.0 0.0 copy-start
  0.0 1.0 %copy-done = bf16[1,1,512,512]{3,2,1,0:T(8,128)(2,1)S(1)} copy-done((bf16[1,1,512,512]{3,2,1,0:T(8,128)(2,1)S(1)}, bf16[1,1,512,512]{3,2,1,0:T(8,128)(2,1)}, u32[]{:S(2)}) %copy-start) | copy-done | bytes 524312
  1.0 0.0 copy-start.1
  1.0 0.9 copy-done.1
  1.9 0.0 copy-start.2
  1.9 0.9 copy-done.2
  2.9 95.0 %shard_map.37 = f32[8,512]{1,0:T(8,128)S(1)} custom-call(bf16[128,512]{1,0:T(8,128)(2,1)S(1)} %bitcast.5, bf16[512,512]{1,0:T(8,128)(2,1)S(1)} %bitcast.4, bf16[128,512]{1,0:T(8,128)(2,1)S(1)} %bitcast.6), custom_call_target="tpu_custom_call" | custom-call | tf_op jit(solution)/shard_map/pallas_call | solution.py:472
  97.9 0.6 copy.5
Async XLA Ops:
  0.0 1.0 %copy-start = (bf16[1,1,512,512]{3,2,1,0:T(8,128)(2,1)S(1)}, bf16[1,1,512,512]{3,2,1,0:T(8,128)(2,1)}, u32[]{:S(2)}) copy-start(bf16[1,1,512,512]{3,2,1,0:T(8,128)(2,1)} %param.4) | copy-start | bytes 1572868
  1.0 0.9 copy-start.1
  1.9 0.9 copy-start.2

commit v5 on v4

--- a/solution.py
+++ b/solution.py
@@ -170,8 +170,8 @@
             for copy in self.copies(phase):
                 copy.start()
 
-    def close(self):
-        for phase in range(5):
+    def close(self, phases):
+        for phase in phases:
             for copy in self.copies(phase):
                 copy.wait_send()
 
@@ -441,13 +441,24 @@
     inverse_refs = (m, ahead, lefts, rights)
     last = at({1: [(weightsums, 3)], 2: [(weightsums, 4)]})
 
+    def close(groups, phases):
+        for group in groups:
+            group.close(phases)
+
+    def close_some():
+        close(acts, range(5))
+        close(gradsums, range(4))
+        close(weightsums, range(2))
+
     def one_by_one():
         step(acts, 5)
         spread(full, 0, m, 0, scale, column)
         inverses(*inverse_refs, at({
             1: [(gradsums, 1), (weightsums, 0)], 2: [(gradsums, 2)], 3: [(gradsums, 3), (weightsums, 1)],
         }), 0, 1)
-        in_order((gradsums, 4), (weightsums, 2), (gradsums, 5))
+        in_order((gradsums, 4), (weightsums, 2))
+        close_some()
+        step(gradsums, 5)
         spread(full, 10, m, 1, scale, None)
         inverses(*inverse_refs, last, 1, 1)
 
@@ -455,17 +466,19 @@
         in_order((gradsums, 1), (acts, 2), (weightsums, 0), (gradsums, 2), (acts, 3), (gradsums, 3), (acts, 4),
                  (weightsums, 1), (gradsums, 4), (acts, 5))
         spread(full, 0, m, 0, scale, column)
-        in_order((weightsums, 2), (gradsums, 5))
+        step(weightsums, 2)
+        close_some()
+        step(gradsums, 5)
         spread(full, 10, m, 1, scale, None)
         inverses(*inverse_refs, last, 0, 2)
 
+    gather.close()
     early(one_by_one)
     late(together)
     step(weightsums, 5)
     finish(m, full, scale, column, place.dp * 8, out_ref)
-    gather.close()
-    for group in acts + gradsums + weightsums:
-        group.close()
+    close(gradsums, range(4, 5))
+    close(weightsums, range(2, 5))
 
 
 def preconditioned(x, w, top):
@@ -500,7 +513,7 @@
             pltpu.SemaphoreType.DMA((3,)),
         ],
         compiler_params=pltpu.CompilerParams(
-            collective_id=0, has_side_effects=True, vmem_limit_bytes=40 << 20
+            collective_id=0, has_side_effects=True, vmem_limit_bytes=64 << 20
         ),
     )(x, w, top)
 

time: 99.1 us -> 98.2 us (level)
  local copies, waits for them, and re-layouts: 3.46 us -> 1.32 us
  Pallas kernels: 95 us -> 96.6 us
    unnamed x7 -> x1, local copies, waits for them, and re-layouts: 3.46 us -> 1.32 us
    pallas_call x1, Pallas kernels: 95 us -> 96.6 us  [preconditioned(): pl.pallas_call(kernel, out_shape=jax.ShapeDtypeStruct((8, 512), F32), in_...]
where the time goes in v5:
time: 98.2 us; the launch traced here: 98 us
  Pallas kernels  96.6 us (98%)
  local copies, waits for them, and re-layouts  1.32 us (1%)
    pallas_call x1, Pallas kernels, preconditioned(): pl.pallas_call(kernel, out_shape=jax.ShapeDtypeStruct((8, 512), F32), in_...  96.6 us

profile of v5, /device:TPU:1, one launch (start us, length us, event | category | flops | bytes accessed | tf_op | source)
XLA Modules:
  0.0 98.0 jit_solution(8635907692792263874)
XLA Ops:
  0.0 96.6 %shard_map.37 = f32[8,512]{1,0:T(8,128)} custom-call(bf16[128,512]{1,0:T(8,128)(2,1)} %bitcast.5, bf16[512,512]{1,0:T(8,128)(2,1)} %bitcast.4, bf16[128,512]{1,0:T(8,128)(2,1)} %bitcast.6), custom_call_target="tpu_custom_call" | custom-call | tf_op jit(solution)/shard_map/pallas_call | solution.py:485
  96.7 1.3 %copy.5 = f32[1,1,8,512]{3,2,1,0:T(8,128)} copy(f32[1,1,8,512]{3,2,1,0:T(8,128)} %bitcast.7) | data formatting | bytes 32768

commit v6 on v5

--- a/solution.py
+++ b/solution.py
@@ -400,7 +400,7 @@
 
     gather.run(beside_gather)
     early(functools.partial(step, acts, 3))
-    lax.fori_loop(0, 8, forward, 0)
+    lax.fori_loop(0, 8, forward, 0, unroll=True)
     early(functools.partial(step, acts, 4))
     late(act_sum)
 
@@ -414,7 +414,7 @@
         ).astype(BF16)
 
     upstream = (top[...].astype(F32) * loss_scale).astype(BF16)
-    lax.fori_loop(0, 8, backward, upstream)
+    lax.fori_loop(0, 8, backward, upstream, unroll=True)
     g = grads[place.section]
     for i in range(4):
         product = transposed_dot(g[:, i * 128:(i + 1) * 128], g[:, i * 128:])

time: 98.2 us -> 96.7 us (0.985)
  Pallas kernels: 96.6 us -> 95.1 us
    pallas_call x1, Pallas kernels: 96.6 us -> 95.1 us  [preconditioned(): pl.pallas_call(kernel, out_shape=jax.ShapeDtypeStruct((8, 512), F32), in_...]
where the time goes in v6:
time: 96.7 us; the launch traced here: 96.5 us
  Pallas kernels  95.1 us (98%)
  local copies, waits for them, and re-layouts  1.32 us (1%)
    pallas_call x1, Pallas kernels, preconditioned(): pl.pallas_call(kernel, out_shape=jax.ShapeDtypeStruct((8, 512), F32), in_...  95.1 us

profile of v6, /device:TPU:1, one launch (start us, length us, event | category | flops | bytes accessed | tf_op | source)
XLA Modules:
  0.0 96.5 jit_solution(453013265226492595)
XLA Ops:
  0.0 95.1 %shard_map.37 = f32[8,512]{1,0:T(8,128)} custom-call(bf16[128,512]{1,0:T(8,128)(2,1)} %bitcast.5, bf16[512,512]{1,0:T(8,128)(2,1)} %bitcast.4, bf16[128,512]{1,0:T(8,128)(2,1)} %bitcast.6), custom_call_target="tpu_custom_call" | custom-call | tf_op jit(solution)/shard_map/pallas_call | solution.py:485
  95.1 1.3 %copy.5 = f32[1,1,8,512]{3,2,1,0:T(8,128)} copy(f32[1,1,8,512]{3,2,1,0:T(8,128)} %bitcast.7) | data formatting | bytes 32768
